TPU v7x, 256 devices: a whole 4x4x8 slice. The times are simulated.
256 devices in a mesh: ctx: 32 (over z, x), head: 8 (over y, core).
Axes of the slice: x: 4, y: 4, z: 8, core: 2. Of those that a mesh axis runs over, the one named last changes fastest.
Arguments:
- inputs: bfloat16 [16384, 6144], P('ctx', 'head'), may hold values from -0.046875 to 0.046875
- query: bfloat16 [16384, 8192], P('ctx', 'head'), may hold values from -0.875 to 0.875
- key_rows: bfloat16 [16384, 8192], P('ctx', 'head'), may hold values from -0.875 to 0.875
- value: bfloat16 [16384, 8192], P('ctx', 'head'), may hold values from -0.875 to 0.875
- grad_out: bfloat16 [16384, 8192], P('ctx', 'head'), may hold values from -0.875 to 0.875
- decay_power: int32 [64], replicated, may hold values from 1 to 2048, as said below
Outputs:
- key_grad: float32 [16384, 8192], P('ctx', 'head')
- value_grad: float32 [16384, 8192], P('ctx', 'head')
- query_weight_grad: float32 [6144, 8192], P('ctx', 'head')
Inputs may be any that keep to these rules, and one draw needn't show every extreme that they name: `decay_power`: every entry is a power of two.
All inputs are finite; a program needn't handle non-finite values.
Results may differ from a plain program's by a relative error of at most 0.02.
Values may be sent and summed in bfloat16 or wider, within the bound.
A program may use at most 192 MiB of HBM per device.

v0:
```python
import math

import jax
import jax.numpy as jnp
from jax import lax
from jax.sharding import PartitionSpec as P

HEAD_DIM = 128
BLOCK = 256


HIGH = lax.Precision.HIGHEST


def decayed_sums(query, key_rows, value, grad_out, rates):
    length = query.shape[0]
    place = jnp.arange(length, dtype=jnp.float32)
    tail = jnp.exp(-rates[None, :] * (length - 1.0 - place)[:, None])
    lead = jnp.exp(-rates[None, :] * place[:, None])
    scaled_key = (key_rows.astype(jnp.float32) * tail[:, :, None]).astype(jnp.bfloat16)
    scaled_query = (query.astype(jnp.float32) * lead[:, :, None]).astype(jnp.bfloat16)
    memory = jnp.einsum("tha,thc->hac", scaled_key, value, preferred_element_type=jnp.float32)
    backing = jnp.einsum("tha,thc->hac", scaled_query, grad_out, preferred_element_type=jnp.float32)
    return (memory, backing)


def block_terms(pieces, rates):
    query, key_rows, value, grad_out = pieces
    size = query.shape[0]
    place = jnp.arange(size, dtype=jnp.float32)
    gap = place[:, None] - place[None, :]
    fade = jnp.where(
        gap[None] >= 0.0, jnp.exp(-rates[:, None, None] * jnp.maximum(gap, 0.0)[None]), 0.0
    )
    score_a = (
        jnp.einsum("tha,sha->hts", grad_out, value, preferred_element_type=jnp.float32) * fade
    ).astype(jnp.bfloat16)
    score_b = (
        jnp.einsum("tha,sha->hts", query, key_rows, preferred_element_type=jnp.float32) * fade
    ).astype(jnp.bfloat16)
    grad_q = jnp.einsum("hts,sha->tha", score_a, key_rows, preferred_element_type=jnp.float32)
    grad_k = jnp.einsum("hts,tha->sha", score_a, query, preferred_element_type=jnp.float32)
    grad_v = jnp.einsum("hts,tha->sha", score_b, grad_out, preferred_element_type=jnp.float32)
    memory, backing = decayed_sums(query, key_rows, value, grad_out, rates)
    return (grad_q, grad_k, grad_v, memory, backing)


def span_grads(query, key_rows, value, grad_out, rates, prefix, suffix):
    length, heads, width = query.shape
    count = length // BLOCK
    blocks = tuple(
        (a.reshape(count, BLOCK, heads, width) for a in (query, key_rows, value, grad_out))
    )
    inner_q, inner_k, inner_v, memories, backings = lax.map(
        lambda pieces: block_terms(pieces, rates), blocks
    )
    step_fade = jnp.exp(-rates * float(BLOCK))[:, None, None]

    def forward(carry, memory):
        return (step_fade * carry + memory, carry)

    def backward(carry, backing):
        return (step_fade * carry + backing, carry)

    unused_a, starts = lax.scan(forward, prefix, memories)
    unused_b, finishes = lax.scan(backward, suffix, backings, reverse=True)
    starts = starts.astype(jnp.bfloat16)
    finishes = finishes.astype(jnp.bfloat16)
    place = jnp.arange(BLOCK, dtype=jnp.float32)
    lead_fade = jnp.exp(-rates[None, :] * (place + 1.0)[:, None])[None, :, :, None]
    back_fade = jnp.exp(-rates[None, :] * (BLOCK - place)[:, None])[None, :, :, None]
    query_b, key_b, value_b, grad_b = blocks
    grad_q = inner_q + lead_fade * jnp.einsum(
        "nhac,nthc->ntha", starts, grad_b, preferred_element_type=jnp.float32
    )
    grad_k = inner_k + back_fade * jnp.einsum(
        "nhac,nthc->ntha", finishes, value_b, preferred_element_type=jnp.float32
    )
    grad_v = inner_v + back_fade * jnp.einsum(
        "nhac,ntha->nthc", finishes, key_b, preferred_element_type=jnp.float32
    )
    shape = (length, heads * width)
    return (
        grad_q.reshape(shape).astype(jnp.bfloat16),
        grad_k.reshape(shape),
        grad_v.reshape(shape),
    )


def local(inputs, query, key_rows, value, grad_out, decay_power):
    heads = query.shape[1] // HEAD_DIM
    length = query.shape[0]
    parts = lax.axis_size("ctx")
    rank = lax.axis_index("ctx")
    group = lax.axis_index("head")
    powers = lax.dynamic_slice_in_dim(decay_power, group * heads, heads)
    rates = powers.astype(jnp.float32) * (math.log(2.0) / (4.0 * length * parts))
    shaped = tuple((a.reshape(length, heads, HEAD_DIM) for a in (query, key_rows, value, grad_out)))
    memory, backing = decayed_sums(shaped[0], shaped[1], shaped[2], shaped[3], rates)
    memory = memory.astype(jnp.bfloat16)
    backing = backing.astype(jnp.bfloat16)
    span_rate = rates[None, :] * float(length)
    piece = lax.all_gather(memory[None], "ctx", axis=0, tiled=True)
    index = jnp.arange(piece.shape[0], dtype=jnp.int32)
    gap = jnp.maximum(rank - 1 - index, 0).astype(jnp.float32)
    weight = jnp.where((index < rank)[:, None], jnp.exp(-span_rate * gap[:, None]), 0.0)
    prefix = jnp.einsum("nh,nhac->hac", weight, piece.astype(jnp.float32), precision=HIGH)
    piece = lax.all_gather(backing[None], "ctx", axis=0, tiled=True)
    index = jnp.arange(piece.shape[0], dtype=jnp.int32)
    gap = jnp.maximum(index - rank - 1, 0).astype(jnp.float32)
    weight = jnp.where((index > rank)[:, None], jnp.exp(-span_rate * gap[:, None]), 0.0)
    suffix = jnp.einsum("nh,nhac->hac", weight, piece.astype(jnp.float32), precision=HIGH)
    whole_in = lax.all_gather(inputs, "head", axis=1, tiled=True)
    grad_q, grad_k, grad_v = span_grads(
        shaped[0], shaped[1], shaped[2], shaped[3], rates, prefix, suffix
    )
    weight_grad = lax.psum_scatter(
        jnp.einsum("td,tc->dc", whole_in, grad_q, preferred_element_type=jnp.float32).astype(
            jnp.bfloat16
        ),
        "ctx",
        scatter_dimension=0,
        tiled=True,
    ).astype(jnp.float32)
    return (grad_k, grad_v, weight_grad)


def solution(mesh):
    placed = (
        P("ctx", "head"),
        P("ctx", "head"),
        P("ctx", "head"),
        P("ctx", "head"),
        P("ctx", "head"),
        P(),
    )
    return jax.shard_map(
        local,
        mesh=mesh,
        in_specs=placed,
        out_specs=(P("ctx", "head"), P("ctx", "head"), P("ctx", "head")),
        check_vma=False,
    )
```

profile of v0, /device:TPU:8, one launch (start us, length us, event | category | flops | bytes accessed | tf_op | source)
XLA Modules:
  0.0 503.8 jit_solution(7443567684066461243)
XLA Ops:
  8.9 2.5 convolution_convert_fusion
  12.8 2.5 convolution_convert_fusion.1
  23.2 25.6 %while.51 = (s32[]{:T(128)}, f32[2,256,8,128]{1,3,2,0:T(8,128)}, f32[2,256,8,128]{1,3,2,0:T(8,128)}, f32[2,256,8,128]{1,3,2,0:T(8,128)}, f32[2,8,128,128]{3,2,1,...) while((s32[]{:T(128)}, f32[2,256,8,128]{1,3,2,0:T(8,128)}, ...), condition=%wide.region_1.2_spmd.clone, body=%wide.region_0.1_spmd.sunk.clone | while | flops 811340032 | bytes 43489680 | solution.py:54
  23.3 1.9 multiply_convert_fusion.18
  28.7 3.1 fusion.122
  36.1 1.9 multiply_convert_fusion.18
  41.6 3.1 fusion.122
  48.8 63.9 %all-gather.10.cloned.1.call-done = bf16[256,128,128]{2,1,0:T(8,128)(2,1)} async-done(((bf16[8,128,128]{2,1,0:T(8,128)(2,1)}), bf16[256,128,128]{2,1,0:T(8,128)(2,1)}) %all-gather.10.cloned.1.call-update) | async-done | bytes 8388624 | tf_op jit(solution)/shard_map/all_gather | solution.py:103
  112.7 11.5 %fusion.38 = f32[8,1,128,128]{3,1,2,0:T(1,128)S(1)} fusion(f32[32,8,1,1]{0,2,3,1:T(1,128)S(1)} %copy.60, bf16[32,8,128,128]{3,2,1,0:T(8,128)(2,1)} %bitcast.234), kind=kOutput, calls=%fused_computation.56 | convolution fusion | flops 50331648 | bytes 8913920 | tf_op jit(solution)/shard_map/nh,nhac->hac/dot_general | solution.py:107
  124.2 2.7 while.53
  126.9 3.0 fusion.43
  129.9 1.7 copy.51
  131.7 22.6 %all-gather.6.cloned.1.call-done = bf16[512,6144]{1,0:T(8,128)(2,1)} async-done(((bf16[512,768]{1,0:T(8,128)(2,1)}), bf16[512,6144]{1,0:T(8,128)(2,1)}) %all-gather.6.cloned.1.call-update) | async-done | bytes 6291472 | tf_op jit(solution)/shard_map/all_gather | solution.py:113
  154.2 12.4 %convert_bitcast_fusion = bf16[6144,1024]{0,1:T(8,128)(2,1)} fusion(bf16[512,6144]{1,0:T(8,128)(2,1)} %all-gather.6.cloned.1.call-done, bf16[64,8,8,128]{3,2,1,0:T(8,128)(2,1)S(1)} %bitcast.250), kind=kOutput, calls=%fused_computation.55 | convolution fusion | flops 6448742400 | bytes 19922944 | tf_op jit(solution)/shard_map/td,tc->dc/dot_general | solution.py:118
  166.6 16.7 %copy.65 = bf16[6144,1024]{1,0:T(8,128)(2,1)} copy(bf16[6144,1024]{0,1:T(8,128)(2,1)} %convert_bitcast_fusion) | data formatting | bytes 25165824
  183.4 72.8 %all-gather.8.cloned.1.call-done = bf16[256,128,128]{2,1,0:T(8,128)(2,1)} async-done(((bf16[8,128,128]{2,1,0:T(8,128)(2,1)}), bf16[256,128,128]{2,1,0:T(8,128)(2,1)}) %all-gather.8.cloned.1.call-update) | async-done | bytes 8388624 | tf_op jit(solution)/shard_map/all_gather | solution.py:108
  256.2 11.5 %fusion.40 = f32[8,1,128,128]{3,1,2,0:T(1,128)S(1)} fusion(f32[32,8,1,1]{0,2,3,1:T(1,128)S(1)} %copy.56, bf16[32,8,128,128]{3,2,1,0:T(8,128)(2,1)} %bitcast.233), kind=kOutput, calls=%fused_computation.58 | convolution fusion | flops 50331648 | bytes 8913920 | tf_op jit(solution)/shard_map/nh,nhac->hac/dot_general | solution.py:112
  267.7 2.6 while.52
  270.4 3.4 fusion.45
  273.7 2.1 copy.44
  275.9 1.8 copy.103
  279.1 1.9 copy.47
  280.9 3.4 copy.102
  284.3 210.7 %reduce-scatter.4.cloned.1.call-done = bf16[192,1024]{1,0:T(8,128)(2,1)} async-done(((bf16[6144,1024]{1,0:T(8,128)(2,1)}), bf16[192,1024]{1,0:T(8,128)(2,1)}) %reduce-scatter.4.cloned.1.call-update) | async-done | bytes 393232
  (119 shorter events, 35.3 us)
Async XLA Ops:
  7.2 105.5 %all-gather.10.cloned.1.call-start = ((), (), s32[]{:S(2)}) async-start(), calls=%async_computation.3 | async-start | bytes 8650752 | tf_op jit(solution)/shard_map/all_gather | solution.py:103
  8.9 3.3 copy-start.15
  11.5 142.8 %all-gather.6.cloned.1.call-start = ((), (), s32[]{:S(2)}) async-start(), calls=%async_computation.1 | async-start | bytes 7077888 | tf_op jit(solution)/shard_map/all_gather | solution.py:113
  12.2 243.9 %all-gather.8.cloned.1.call-start = ((), (), s32[]{:S(2)}) async-start(), calls=%async_computation.2 | async-start | bytes 8650752 | tf_op jit(solution)/shard_map/all_gather | solution.py:108
  12.8 2.6 copy-start.14
  15.4 479.7 %reduce-scatter.4.cloned.1.call-start = ((), (), s32[]{:S(2)}) async-start(), calls=%async_computation.4 | async-start | bytes 12976128
  16.7 1.6 copy-start.18
  18.4 2.5 copy-start.16
  23.2 2.0 copy-start
  23.2 2.0 copy-start.2
  28.7 3.2 copy-start.10
  28.7 4.5 copy-start.12
  33.3 1.7 copy-start.11
  36.0 2.0 copy-start
  36.0 2.0 copy-start.2
  41.6 3.2 copy-start.10
  41.6 4.5 copy-start.12
  46.0 1.7 copy-start.11
  112.7 11.5 %copy-start.9 = (bf16[2,8,128,128]{3,2,1,0:T(8,128)(2,1)S(1)}, bf16[2,8,128,128]{3,2,1,0:T(8,128)(2,1)}, u32[]{:S(2)}) copy-start(bf16[2,8,128,128]{3,2,1,0:T(8,128)(2,1)} %copy-done.7) | copy-start | bytes 1572868
  124.2 2.7 copy-start.6
  256.2 11.5 %copy-start.8 = (bf16[2,8,128,128]{3,2,1,0:T(8,128)(2,1)S(1)}, bf16[2,8,128,128]{3,2,1,0:T(8,128)(2,1)}, u32[]{:S(2)}) copy-start(bf16[2,8,128,128]{3,2,1,0:T(8,128)(2,1)} %copy-done.7) | copy-start | bytes 1572868
  267.7 2.7 copy-start.4
  275.8 1.8 copy-start.1
  275.8 2.7 copy-start.19
  (7 other events, 8.1 us)
Sparse Core Ops, SparseCore 0:
  11.6 101.0 all-gather.9
  114.5 39.6 all-gather.5
  156.8 99.2 all-gather.7
  260.2 234.8 reduce-scatter.3
where the time goes:
time: 505 us; the launch traced here: 504 us
  waiting for transfers between devices  371 us (73%)
  matrix products  68.8 us (14%)
  local copies, waits for them, and re-layouts  43.9 us (9%)
  between operations  14.1 us (3%)
  other arithmetic  5.9 us (1%)
    unnamed x5, waiting for transfers between devices  211 us
    all_gather x1, waiting for transfers between devices, local(): piece = lax.all_gather(backing[None], 'ctx', axis=0, tiled=True)  72.8 us
    all_gather x1, waiting for transfers between devices, local(): piece = lax.all_gather(memory[None], 'ctx', axis=0, tiled=True)  63.9 us
    unnamed x39, local copies, waits for them, and re-layouts  29.8 us
    dot_general x2, matrix products, local(): jnp.einsum('nh,nhac->hac', weight, piece.astype(jnp.float32), precision=H...  23 us
    all_gather x1, waiting for transfers between devices, local(): whole_in = lax.all_gather(inputs, 'head', axis=1, tiled=True)  22.6 us
    dot_general x1, matrix products, local(): jnp.einsum('td,tc->dc', whole_in, grad_q, preferred_element_type=jnp.floa...  12.4 us
  transfers between devices with their start and end apart: 4, of which 4 were waited for; matrix products, arithmetic and copies ran while one was open for 21% of the time, Pallas kernels for 0%

commit v1 on v0

v1 whole, which is shorter than its diff:
```python
import math

import jax
import jax.numpy as jnp
from jax import lax
from jax.experimental import pallas as pl
from jax.experimental.pallas import tpu as pltpu
from jax.sharding import PartitionSpec as P

X, Z, Y = 4, 8, 4
W = 128
B = 256
T = 2 * B
H = 8
G = 2
HG = H // G
Q = W // X
F = 192
FEATURES = F * Z
MESH = pl.DeviceIdType.MESH
F32, BF16 = jnp.float32, jnp.bfloat16
MEM, BACK = 0, 1


def dot(a, b, ca, cb):
    return lax.dot_general(a, b, (((ca,), (cb,)), ((), ())), preferred_element_type=F32)


def rcopy(src, dst, ss, rs, dev):
    return pltpu.make_async_remote_copy(
        src_ref=src, dst_ref=dst, send_sem=ss, recv_sem=rs, device_id=dev, device_id_type=MESH
    )


def kernel(
    x_hbm, q_hbm, k_hbm, v_hbm, g_hbm, power,
    key_out, value_out, weight_out,
    xin, qv, kv, vv, gv, xown, xt,
    bm0, bb1, memq, s1, lz, gz, out3, p3,
    qi, kg, vg, qg, part, sb, rb, wout,
    ld, xl, xs_s, xs_r, ys_s, ys_r, cs_s, cs_r,
    s1_s, s1_r, s2_s, s2_r, s3_s, s3_r, qg_s, qg_r, rs_s, rs_r, kv_o, w_o,
):
    ctx = lax.axis_index("ctx")
    hd = lax.axis_index("head")
    x, z = lax.rem(ctx, X), ctx // X
    y, core = hd // 2, lax.rem(hd, 2)

    def at_x(d):
        return (z * X + lax.rem(x + d, X), hd)

    def at_z(zt):
        return (zt * X + x, hd)

    def at_y(d):
        return (ctx, lax.rem(y + d, Y) * 2 + core)

    sibling = (ctx, y * 2 + 1 - core)

    loads = [
        pltpu.make_async_copy(src, dst, ld.at[i])
        for i, (src, dst) in enumerate(
            ((k_hbm, kv), (v_hbm, vv), (x_hbm, xin), (q_hbm, qv), (g_hbm, gv))
        )
    ]
    for c in loads:
        c.start()

    barrier = pltpu.get_barrier_semaphore()
    partners = (
        [at_x(d) for d in range(1, X)]
        + [at_z(lax.rem(z + d, Z)) for d in range(1, Z)]
        + [at_y(d) for d in range(1, Y)]
        + [sibling]
    )
    for dev in partners:
        pl.semaphore_signal(barrier, inc=1, device_id=dev, device_id_type=MESH)

    def rate_of(h):
        return power[hd * H + h].astype(F32) * (math.log(2.0) / (4.0 * T * X * Z))

    def decay(rate, count):
        return jnp.exp(jnp.full((1, W), -rate * count, F32))

    def rows():
        return lax.broadcasted_iota(jnp.int32, (B, W), 0).astype(F32)

    def cols(h):
        return pl.ds(pl.multiple_of(h * W, W), W)

    def mem_head(h, carry):
        rate = rate_of(h)
        tail = jnp.exp(-rate * ((B - 1.0) - rows()))
        sums = []
        for b in range(2):
            r = pl.ds(b * B, B)
            low = (kv[r, cols(h)].astype(F32) * tail).astype(BF16)
            sums.append(dot(low, vv[r, cols(h)], 0, 0))
        bm0[h] = sums[0]
        m = (decay(rate, float(B)) * sums[0] + sums[1]).astype(BF16)
        for i in range(X):
            memq[MEM, i, h] = m[i * Q : (i + 1) * Q]
        return carry

    def back_head(h, carry):
        rate = rate_of(h)
        lead = jnp.exp(-rate * rows())
        sums = []
        for b in range(2):
            r = pl.ds(b * B, B)
            low = (qv[r, cols(h)].astype(F32) * lead).astype(BF16)
            sums.append(dot(low, gv[r, cols(h)], 0, 0))
        bb1[h] = sums[1]
        m = (sums[0] + decay(rate, float(B)) * sums[1]).astype(BF16)
        for i in range(X):
            memq[BACK, i, h] = m[i * Q : (i + 1) * Q]
        return carry

    def heads(g):
        return pl.ds(g * HG, HG)

    def stage1(kind, g, d):
        xt_to = lax.rem(x + d, X)
        return rcopy(
            memq.at[kind, xt_to, heads(g)], s1.at[kind, x, heads(g)],
            s1_s.at[kind, g, d - 1], s1_r.at[kind, g, d - 1], at_x(d),
        )

    def stage1_recv(kind, g, d):
        xf = lax.rem(x - d + X, X)
        dst = s1.at[kind, xf, heads(g)]
        rcopy(dst, dst, s1_s.at[kind, g, d - 1], s1_r.at[kind, g, d - 1], at_x(d)).wait_recv()

    def send_stage1(kind):
        s1[kind, x] = memq[kind, x]
        for g in range(G):
            for d in (1, 3, 2):
                stage1(kind, g, d).start()

    def stage2(kind, g, zt):
        return rcopy(
            lz.at[kind, heads(g)], gz.at[z, heads(g)], s2_s.at[g, zt], s2_r.at[g, z], at_z(zt)
        )

    def line_sums(kind, g):
        for d in range(1, X):
            stage1_recv(kind, g, d)

        def one(i, carry):
            h = g * HG + i
            d = decay(rate_of(h), float(T))
            order = range(X) if kind == MEM else range(X - 1, -1, -1)
            total = None
            for xi in order:
                term = s1[kind, xi, h].astype(F32)
                total = term if total is None else total * d + term
            lz[kind, h] = total.astype(BF16)
            return carry

        lax.fori_loop(0, HG, one, 0)

        def send(i, carry):
            zt = z + 1 + i if kind == MEM else z - 1 - i
            stage2(kind, g, zt).start()
            return carry

        lax.fori_loop(0, Z - 1 - z if kind == MEM else z, send, 0)

    def stage3(kind, g, d):
        xt_to = lax.rem(x + d, X)
        return rcopy(
            out3.at[kind, xt_to, heads(g)], p3.at[kind, x, heads(g)],
            s3_s.at[kind, g, d - 1], s3_r.at[kind, g, d - 1], at_x(d),
        )

    def stage3_recv(kind, g, d):
        xf = lax.rem(x - d + X, X)
        dst = p3.at[kind, xf, heads(g)]
        rcopy(dst, dst, s3_s.at[kind, g, d - 1], s3_r.at[kind, g, d - 1], at_x(d)).wait_recv()

    def scans(kind, g):
        count = z if kind == MEM else Z - 1 - z

        def source(i):
            return i if kind == MEM else Z - 1 - i

        def wait(i, carry):
            dst = gz.at[source(i), heads(g)]
            rcopy(dst, dst, s2_s.at[g, 0], s2_r.at[g, source(i)], at_z(source(i))).wait_recv()
            return carry

        lax.fori_loop(0, count, wait, 0)

        def one(i, carry):
            h = g * HG + i
            rate = rate_of(h)
            d, line = decay(rate, float(T)), decay(rate, float(T * X))

            def add(i, total):
                return total * line + gz[source(i), h].astype(F32)

            run = lax.fori_loop(0, count, add, jnp.zeros((Q, W), F32))
            order = range(X) if kind == MEM else range(X - 1, -1, -1)
            for xi in order:
                out3[kind, xi, h] = run.astype(BF16)
                run = run * d + s1[kind, xi, h].astype(F32)
            return carry

        lax.fori_loop(0, HG, one, 0)
        p3[kind, x, heads(g)] = out3[kind, x, heads(g)]
        for d in (1, 3, 2):
            stage3(kind, g, d).start()

    def inner_head(h, carry):
        rate = rate_of(h)
        t = lax.broadcasted_iota(jnp.int32, (B, B), 0)
        s = lax.broadcasted_iota(jnp.int32, (B, B), 1)
        gap = (t - s).astype(F32)
        fade = jnp.where(gap >= 0.0, jnp.exp(-rate * jnp.maximum(gap, 0.0)), 0.0)
        turned = jnp.where(gap <= 0.0, jnp.exp(rate * jnp.minimum(gap, 0.0)), 0.0)
        for b in range(2):
            r = pl.ds(b * B, B)
            qh, kh, vh, gh = (a[r, cols(h)] for a in (qv, kv, vv, gv))
            sa = (dot(gh, vh, 1, 1) * fade).astype(BF16)
            qi[h, r] = dot(sa, kh, 1, 0)
            sat = (dot(vh, gh, 1, 1) * turned).astype(BF16)
            kg[h, r] = dot(sat, qh, 1, 0)
            sbt = (dot(kh, qh, 1, 1) * turned).astype(BF16)
            vg[h, r] = dot(sbt, gh, 1, 0)
        return carry

    def qg_send(h, d):
        mine = qg.at[h, pl.ds(pl.multiple_of(x * T, T), T)]
        return rcopy(mine, mine, qg_s.at[h, d - 1], qg_r.at[h, d - 1], at_x(d))

    def qg_recv(h, d):
        xf = lax.rem(x - d + X, X)
        dst = qg.at[h, pl.ds(pl.multiple_of(xf * T, T), T)]
        rcopy(dst, dst, qg_s.at[h, d - 1], qg_r.at[h, d - 1], at_x(d)).wait_recv()

    def query_head(h, carry):
        rate = rate_of(h)
        lead = jnp.exp(-rate * (rows() + 1.0))
        prefix = p3[MEM, :, h].reshape(W, W)
        starts = (prefix, (decay(rate, float(B)) * prefix.astype(F32) + bm0[h]).astype(BF16))
        for b in range(2):
            r = pl.ds(b * B, B)
            whole = qi[h, r] + lead * dot(gv[r, cols(h)], starts[b], 1, 1)
            qg[h, pl.ds(pl.multiple_of(x * T + b * B, B), B)] = whole.astype(BF16)
        for d in (1, 3, 2):
            qg_send(h, d).start()
        return carry

    def kv_copies(h):
        return (
            pltpu.make_async_copy(kg.at[h], key_out.at[:, cols(h)], kv_o.at[0, h]),
            pltpu.make_async_copy(vg.at[h], value_out.at[:, cols(h)], kv_o.at[1, h]),
        )

    def key_value_head(h, carry):
        rate = rate_of(h)
        fall = jnp.exp(-rate * (float(B) - rows()))
        suffix = p3[BACK, :, h].reshape(W, W)
        finishes = ((decay(rate, float(B)) * suffix.astype(F32) + bb1[h]).astype(BF16), suffix)
        for b in range(2):
            r = pl.ds(b * B, B)
            kg[h, r] += fall * dot(vv[r, cols(h)], finishes[b], 1, 1)
            vg[h, r] += fall * dot(kv[r, cols(h)], finishes[b], 1, 0)
        for c in kv_copies(h):
            c.start()
        return carry

    def x_rows(owner):
        return pl.ds(pl.multiple_of(owner * F, F), F)

    def x_cols(xi):
        return pl.ds(pl.multiple_of(xi * T, T), T)

    def x_send(d):
        return rcopy(
            xown.at[lax.rem(x + d, X)], xt.at[x_rows(hd), x_cols(x)],
            xs_s.at[d - 1], xs_r.at[d - 1], at_x(d),
        )

    def x_recv(d):
        xf = lax.rem(x - d + X, X)
        dst = xt.at[x_rows(hd), x_cols(xf)]
        rcopy(dst, dst, xs_s.at[d - 1], xs_r.at[d - 1], at_x(d)).wait_recv()

    def y_send(xi, d):
        mine = xt.at[x_rows(hd), x_cols(xi)]
        return rcopy(mine, mine, ys_s.at[xi, d - 1], ys_r.at[xi, d - 1], at_y(d))

    def y_recv(xi, d):
        owner = lax.rem(y - d + Y, Y) * 2 + core
        dst = xt.at[x_rows(owner), x_cols(xi)]
        rcopy(dst, dst, ys_s.at[xi, d - 1], ys_r.at[xi, d - 1], at_y(d)).wait_recv()

    def core_send(d):
        mine = xt.at[x_rows(lax.rem(y - d + Y, Y) * 2 + core)]
        return rcopy(mine, mine, cs_s.at[d], cs_r.at[d], sibling)

    def core_recv(d):
        dst = xt.at[x_rows(lax.rem(y - d + Y, Y) * 2 + 1 - core)]
        rcopy(dst, dst, cs_s.at[d], cs_r.at[d], sibling).wait_recv()

    loads[0].wait()
    loads[1].wait()
    lax.fori_loop(0, H, mem_head, 0)
    loads[2].wait()
    for i in range(X):
        xown[i] = xin[:, i * F : (i + 1) * F].T
    pl.semaphore_wait(barrier, len(partners))
    send_stage1(MEM)
    own = pltpu.make_async_copy(xown.at[x], xt.at[x_rows(hd), x_cols(x)], xl)
    own.start()
    for d in (1, 3, 2):
        x_send(d).start()
    own.wait()
    for d in (1, 3, 2):
        y_send(x, d).start()
    loads[3].wait()
    loads[4].wait()
    lax.fori_loop(0, H, back_head, 0)
    send_stage1(BACK)
    for g in range(G):
        line_sums(MEM, g)
    for g in range(G):
        line_sums(BACK, g)
    lax.fori_loop(0, H // 2, inner_head, 0)
    for d in (1, 3, 2):
        x_recv(d)
        for e in (1, 3, 2):
            y_send(lax.rem(x - d + X, X), e).start()
    core_send(0).start()
    for g in range(G):
        scans(MEM, g)
    lax.fori_loop(H // 2, H, inner_head, 0)
    for g in range(G):
        for d in range(1, X):
            stage3_recv(MEM, g, d)
        lax.fori_loop(g * HG, (g + 1) * HG, query_head, 0)
    for g in range(G):
        scans(BACK, g)
    for g in range(G):
        for d in range(1, X):
            stage3_recv(BACK, g, d)
        lax.fori_loop(g * HG, (g + 1) * HG, key_value_head, 0)
    for d in (1, 3, 2):
        for xi in range(X):
            y_recv(xi, d)
        core_send(d).start()
    for d in range(Y):
        core_recv(d)

    def hops(j, way):
        odd = lax.rem(j, 2)
        return Z // 2 - 1 + odd if way == 0 else Z // 2 - odd

    def block(j, zt):
        return part[j, x_rows(lax.rem(zt + Z, Z))]

    def ring(j, way, s):
        zt = lax.rem(z + 1, Z) if way == 0 else lax.rem(z + Z - 1, Z)
        return rcopy(
            sb.at[j, way, s], rb.at[j, way, s], rs_s.at[j, way, s], rs_r.at[j, way, s], at_z(zt)
        )

    def target(j, way, s):
        left = hops(j, way) - s
        return z + left if way == 0 else z - left

    def weight_copy(j):
        return pltpu.make_async_copy(wout.at[j], weight_out.at[:, cols(j)], w_o.at[j])

    def slot(t, carry):
        @pl.when(t < H)
        def _():
            for d in range(1, X):
                qg_recv(t, d)
            for i in range(2):
                r = pl.ds(i * (FEATURES // 2), FEATURES // 2)
                part[t, r] = dot(xt[r, :], qg[t], 1, 0)
            for way in range(2):
                sb[t, way, 0] = block(t, target(t, way, 0)).astype(BF16)
                ring(t, way, 0).start()

        for s in range(1, Z // 2):
            j = t - s

            @pl.when((j >= 0) & (j < H))
            def _():
                for way in range(2):
                    @pl.when(s < hops(j, way))
                    def _():
                        ring(j, way, s - 1).wait_recv()
                        total = rb[j, way, s - 1].astype(F32) + block(j, target(j, way, s))
                        sb[j, way, s] = total.astype(BF16)
                        ring(j, way, s).start()

        last = t - Z // 2

        @pl.when(last >= 0)
        def _():
            total = block(last, z)
            for way in range(2):
                s = hops(last, way) - 1
                ring(last, way, s).wait_recv()
                total += rb[last, way, s].astype(F32)
            wout[last] = total
            weight_copy(last).start()

        return carry

    lax.fori_loop(0, H + Z // 2, slot, 0)

    def drain(h, carry):
        for d in range(1, X):
            qg_send(h, d).wait_send()
        for way in range(2):
            for s in range(Z // 2):
                @pl.when(s < hops(h, way))
                def _():
                    ring(h, way, s).wait_send()
        for c in kv_copies(h):
            c.wait()
        weight_copy(h).wait()
        return carry

    lax.fori_loop(0, H, drain, 0)
    for d in range(1, X):
        x_send(d).wait_send()
        for kind in range(2):
            for g in range(G):
                stage1(kind, g, d).wait_send()
                stage3(kind, g, d).wait_send()
    for d in range(1, Y):
        for xi in range(X):
            y_send(xi, d).wait_send()
    for d in range(Y):
        core_send(d).wait_send()
    for g in range(G):
        def up(zt, carry):
            stage2(MEM, g, zt).wait_send()
            return carry

        def down(zt, carry):
            stage2(BACK, g, zt).wait_send()
            return carry

        lax.fori_loop(z + 1, Z, up, 0)
        lax.fori_loop(0, z, down, 0)


def local(inputs, query, key_rows, value, grad_out, decay_power):
    dma = pltpu.SemaphoreType.DMA
    anywhere = pl.BlockSpec(memory_space=pl.ANY)
    return pl.pallas_call(
        kernel,
        out_shape=(
            jax.ShapeDtypeStruct((T, H * W), F32),
            jax.ShapeDtypeStruct((T, H * W), F32),
            jax.ShapeDtypeStruct((F, H * W), F32),
        ),
        in_specs=[anywhere] * 5 + [pl.BlockSpec(memory_space=pltpu.SMEM)],
        out_specs=(anywhere,) * 3,
        scratch_shapes=[
            pltpu.VMEM((T, X * F), BF16),
            pltpu.VMEM((T, H * W), BF16),
            pltpu.VMEM((T, H * W), BF16),
            pltpu.VMEM((T, H * W), BF16),
            pltpu.VMEM((T, H * W), BF16),
            pltpu.VMEM((X, F, T), BF16),
            pltpu.VMEM((FEATURES, X * T), BF16),
            pltpu.VMEM((H, W, W), F32),
            pltpu.VMEM((H, W, W), F32),
            pltpu.VMEM((2, X, H, Q, W), BF16),
            pltpu.VMEM((2, X, H, Q, W), BF16),
            pltpu.VMEM((2, H, Q, W), BF16),
            pltpu.VMEM((Z, H, Q, W), BF16),
            pltpu.VMEM((2, X, H, Q, W), BF16),
            pltpu.VMEM((2, X, H, Q, W), BF16),
            pltpu.VMEM((H, T, W), F32),
            pltpu.VMEM((H, T, W), F32),
            pltpu.VMEM((H, T, W), F32),
            pltpu.VMEM((H, X * T, W), BF16),
            pltpu.VMEM((H, FEATURES, W), F32),
            pltpu.VMEM((H, 2, Z // 2, F, W), BF16),
            pltpu.VMEM((H, 2, Z // 2, F, W), BF16),
            pltpu.VMEM((H, F, W), F32),
            dma((5,)),
            dma,
            dma((X - 1,)),
            dma((X - 1,)),
            dma((X, Y - 1)),
            dma((X, Y - 1)),
            dma((Y,)),
            dma((Y,)),
            dma((2, G, X - 1)),
            dma((2, G, X - 1)),
            dma((G, Z)),
            dma((G, Z)),
            dma((2, G, X - 1)),
            dma((2, G, X - 1)),
            dma((H, X - 1)),
            dma((H, X - 1)),
            dma((H, 2, Z // 2)),
            dma((H, 2, Z // 2)),
            dma((2, H)),
            dma((H,)),
        ],
        compiler_params=pltpu.CompilerParams(
            collective_id=0, has_side_effects=True, vmem_limit_bytes=60 * 2**20
        ),
        cost_estimate=pl.CostEstimate(
            flops=9 * 10**9, bytes_accessed=10 * 2**20, transcendentals=10**6
        ),
    )(inputs, query, key_rows, value, grad_out, decay_power)


def solution(mesh):
    placed = (P("ctx", "head"),) * 5 + (P(),)
    return jax.shard_map(
        local,
        mesh=mesh,
        in_specs=placed,
        out_specs=(P("ctx", "head"),) * 3,
        check_vma=False,
    )
```

time: 505 us -> 139 us (0.28)
  waiting for transfers between devices: 371 us -> 0 us
  Pallas kernels: 0 us -> 130 us
  matrix products: 68.8 us -> 0 us
  local copies, waits for them, and re-layouts: 43.9 us -> 5.87 us
  between operations: 14.1 us -> 0.65 us
  other arithmetic: 5.9 us -> 0 us
    unnamed x5 -> x0, waiting for transfers between devices: 211 us -> none
    all_gather x3 -> x0, waiting for transfers between devices: 159 us -> none  [the longest x1 72.8 us: local(): piece = lax.all_gather(backing[None], 'ctx', axis=0, tiled=True)]
    pallas_call x0 -> x1, Pallas kernels: none -> 130 us  [local(): pl.pallas_call(kernel, out_shape=(jax.ShapeDtypeStruct((T, H * W), F32),...]
    dot_general x20 -> x0, matrix products: 68.8 us -> none  [the longest x2 23 us: local(): jnp.einsum('nh,nhac->hac', weight, piece.astype(jnp.float32), precision=H...]
    unnamed x39 -> x7, local copies, waits for them, and re-layouts: 29.8 us -> 5.87 us
  transfers between devices with their start and end apart: 4 -> 0, of which waited for: 4 -> 0; matrix products, arithmetic and copies ran while one was open for 21% -> 0% of each run, Pallas kernels for 0% -> 0%
where the time goes in v1:
time: 139 us; the launch traced here: 137 us
  Pallas kernels  130 us (94%)
  local copies, waits for them, and re-layouts  5.87 us (4%)
    pallas_call x1, Pallas kernels, local(): pl.pallas_call(kernel, out_shape=(jax.ShapeDtypeStruct((T, H * W), F32),...  130 us
    unnamed x7, local copies, waits for them, and re-layouts  5.87 us

profile of v1, /device:TPU:8, one launch (start us, length us, event | category | flops | bytes accessed | tf_op | source)
XLA Modules:
  0.0 136.9 jit_solution(12525077683588994459)
XLA Ops:
  0.6 130.4 %shard_map.85 = (f32[512,1024]{1,0:T(8,128)}, f32[512,1024]{1,0:T(8,128)}, f32[192,1024]{1,0:T(8,128)}) custom-call(bf16[512,768]{1,0:T(8,128)(2,1)} %x_hbm.1, bf16[512,1024]{1,0:T(8,128)(2,1)} %q_hbm.1, bf16[512,1024]{1,0:T(8,128)(2,1)} %k_hbm.1, bf16[512,1024]{1,0:T(8,128)(2,1)} %v_hbm.1, bf16[512,1024]{1,0:T(8,128)(2,1)} %g_hbm.1, s32[64]{0:T(128)} %power.1), custom_call_target="tpu_custom_call" | custom-call | flops 8999999488 | bytes 10485760 | tf_op jit(solution)/shard_map/pallas_call | solution.py:458
  131.0 0.0 copy-start
  131.0 3.3 %copy.12 = f32[512,1024]{1,0:T(8,128)} copy(f32[512,1024]{1,0:T(8,128)} %get-tuple-element.6) | data formatting | bytes 4194304
  134.3 0.0 copy-done
  134.3 0.0 copy-start.1
  134.3 1.3 copy.13
  135.7 0.4 copy-done.1
  136.0 0.9 copy.14
Async XLA Ops:
  131.0 3.3 %copy-start = (f32[512,1024]{1,0:T(8,128)S(1)}, f32[512,1024]{1,0:T(8,128)}, u32[]{:S(2)}) copy-start(f32[512,1024]{1,0:T(8,128)} %get-tuple-element.7) | copy-start | bytes 6291460
  134.3 1.7 %copy-start.1 = (f32[192,1024]{1,0:T(8,128)S(1)}, f32[192,1024]{1,0:T(8,128)}, u32[]{:S(2)}) copy-start(f32[192,1024]{1,0:T(8,128)} %get-tuple-element.8) | copy-start | bytes 2359300

commit v2 on v1

--- a/solution.py
+++ b/solution.py
@@ -20,6 +20,8 @@
 MESH = pl.DeviceIdType.MESH
 F32, BF16 = jnp.float32, jnp.bfloat16
 MEM, BACK = 0, 1
+LEAD = 2
+FIRST = 2
 
 
 def dot(a, b, ca, cb):
@@ -35,11 +37,11 @@
 def kernel(
     x_hbm, q_hbm, k_hbm, v_hbm, g_hbm, power,
     key_out, value_out, weight_out,
-    xin, qv, kv, vv, gv, xown, xt,
+    xin, qv, kv, vv, gv, xown, xt, fades,
     bm0, bb1, memq, s1, lz, gz, out3, p3,
-    qi, kg, vg, qg, part, sb, rb, wout,
-    ld, xl, xs_s, xs_r, ys_s, ys_r, cs_s, cs_r,
-    s1_s, s1_r, s2_s, s2_r, s3_s, s3_r, qg_s, qg_r, rs_s, rs_r, kv_o, w_o,
+    qi, kg, vg, kgo, vgo, qg, part, sb, rb, wout,
+    ld, xl, xs_s, xs_r, ys_s, ys_r, yf_s, yf_r, cs_s, cs_r,
+    s1_s, s1_r, s2_s, s2_r, s3_s, s3_r, qg_s, qg_r, qf_s, qf_r, rs_s, rs_r, kv_o, w_o,
 ):
     ctx = lax.axis_index("ctx")
     hd = lax.axis_index("head")
@@ -86,7 +88,16 @@
         return lax.broadcasted_iota(jnp.int32, (B, W), 0).astype(F32)
 
     def cols(h):
+        if isinstance(h, int):
+            return pl.ds(h * W, W)
         return pl.ds(pl.multiple_of(h * W, W), W)
+
+    for h in range(H):
+        for i, count in enumerate((T, T * X)):
+            fades[i, h] = jnp.exp(jnp.full((8, W), -rate_of(h) * float(count), F32))
+
+    def keep(i, g):
+        return fades[i, g * HG : (g + 1) * HG, 0:1]
 
     def mem_head(h, carry):
         rate = rate_of(h)
@@ -146,18 +157,12 @@
         for d in range(1, X):
             stage1_recv(kind, g, d)
 
-        def one(i, carry):
-            h = g * HG + i
-            d = decay(rate_of(h), float(T))
-            order = range(X) if kind == MEM else range(X - 1, -1, -1)
-            total = None
-            for xi in order:
-                term = s1[kind, xi, h].astype(F32)
-                total = term if total is None else total * d + term
-            lz[kind, h] = total.astype(BF16)
-            return carry
-
-        lax.fori_loop(0, HG, one, 0)
+        d = keep(0, g)
+        total = None
+        for xi in range(X) if kind == MEM else range(X - 1, -1, -1):
+            term = s1[kind, xi, g * HG : (g + 1) * HG].astype(F32)
+            total = term if total is None else total * d + term
+        lz[kind, g * HG : (g + 1) * HG] = total.astype(BF16)
 
         def send(i, carry):
             zt = z + 1 + i if kind == MEM else z - 1 - i
@@ -184,29 +189,18 @@
         def source(i):
             return i if kind == MEM else Z - 1 - i
 
-        def wait(i, carry):
+        line_fade = keep(1, g)
+
+        def add(i, total):
             dst = gz.at[source(i), heads(g)]
             rcopy(dst, dst, s2_s.at[g, 0], s2_r.at[g, source(i)], at_z(source(i))).wait_recv()
-            return carry
-
-        lax.fori_loop(0, count, wait, 0)
-
-        def one(i, carry):
-            h = g * HG + i
-            rate = rate_of(h)
-            d, line = decay(rate, float(T)), decay(rate, float(T * X))
-
-            def add(i, total):
-                return total * line + gz[source(i), h].astype(F32)
-
-            run = lax.fori_loop(0, count, add, jnp.zeros((Q, W), F32))
-            order = range(X) if kind == MEM else range(X - 1, -1, -1)
-            for xi in order:
-                out3[kind, xi, h] = run.astype(BF16)
-                run = run * d + s1[kind, xi, h].astype(F32)
-            return carry
-
-        lax.fori_loop(0, HG, one, 0)
+            return total * line_fade + gz[source(i), g * HG : (g + 1) * HG].astype(F32)
+
+        run = lax.fori_loop(0, count, add, jnp.zeros((HG, Q, W), F32))
+        d = keep(0, g)
+        for xi in range(X) if kind == MEM else range(X - 1, -1, -1):
+            out3[kind, xi, g * HG : (g + 1) * HG] = run.astype(BF16)
+            run = run * d + s1[kind, xi, g * HG : (g + 1) * HG].astype(F32)
         p3[kind, x, heads(g)] = out3[kind, x, heads(g)]
         for d in (1, 3, 2):
             stage3(kind, g, d).start()
@@ -229,14 +223,26 @@
             vg[h, r] = dot(sbt, gh, 1, 0)
         return carry
 
-    def qg_send(h, d):
-        mine = qg.at[h, pl.ds(pl.multiple_of(x * T, T), T)]
-        return rcopy(mine, mine, qg_s.at[h, d - 1], qg_r.at[h, d - 1], at_x(d))
-
-    def qg_recv(h, d):
-        xf = lax.rem(x - d + X, X)
-        dst = qg.at[h, pl.ds(pl.multiple_of(xf * T, T), T)]
-        rcopy(dst, dst, qg_s.at[h, d - 1], qg_r.at[h, d - 1], at_x(d)).wait_recv()
+    def line(xi, half=None):
+        if half is None:
+            return pl.ds(pl.multiple_of(lax.rem(xi + X, X) * T, T), T)
+        return pl.ds(pl.multiple_of(lax.rem(xi + X, X) * T + half * B, B), B)
+
+    def qg_send(h, way):
+        mine = qg.at[h, line(x)]
+        return rcopy(mine, mine, qg_s.at[h, way], qg_r.at[h, way], at_x(X - 1 if way else 1))
+
+    def qg_recv(h, way):
+        dst = qg.at[h, line(x + 1 if way else x - 1)]
+        rcopy(dst, dst, qg_s.at[h, way], qg_r.at[h, way], at_x(1)).wait_recv()
+
+    def qg_pass(h, way):
+        got = qg.at[h, line(x + 1 if way else x - 1, way)]
+        return rcopy(got, got, qf_s.at[h, way], qf_r.at[h, way], at_x(X - 1 if way else 1))
+
+    def qg_pass_recv(h, way):
+        dst = qg.at[h, line(x + 2, way)]
+        rcopy(dst, dst, qf_s.at[h, way], qf_r.at[h, way], at_x(1)).wait_recv()
 
     def query_head(h, carry):
         rate = rate_of(h)
@@ -246,15 +252,17 @@
         for b in range(2):
             r = pl.ds(b * B, B)
             whole = qi[h, r] + lead * dot(gv[r, cols(h)], starts[b], 1, 1)
-            qg[h, pl.ds(pl.multiple_of(x * T + b * B, B), B)] = whole.astype(BF16)
-        for d in (1, 3, 2):
-            qg_send(h, d).start()
+            qg[h, line(x, b)] = whole.astype(BF16)
+        if h < LEAD:
+            for way in range(2):
+                qg_send(h, way).start()
+
         return carry
 
     def kv_copies(h):
         return (
-            pltpu.make_async_copy(kg.at[h], key_out.at[:, cols(h)], kv_o.at[0, h]),
-            pltpu.make_async_copy(vg.at[h], value_out.at[:, cols(h)], kv_o.at[1, h]),
+            pltpu.make_async_copy(kgo.at[h], key_out.at[:, cols(h)], kv_o.at[0, h]),
+            pltpu.make_async_copy(vgo.at[h], value_out.at[:, cols(h)], kv_o.at[1, h]),
         )
 
     def key_value_head(h, carry):
@@ -264,8 +272,8 @@
         finishes = ((decay(rate, float(B)) * suffix.astype(F32) + bb1[h]).astype(BF16), suffix)
         for b in range(2):
             r = pl.ds(b * B, B)
-            kg[h, r] += fall * dot(vv[r, cols(h)], finishes[b], 1, 1)
-            vg[h, r] += fall * dot(kv[r, cols(h)], finishes[b], 1, 0)
+            kgo[h, r] = (kg[h, r] + fall * dot(vv[r, cols(h)], finishes[b], 1, 1)).astype(BF16)
+            vgo[h, r] = (vg[h, r] + fall * dot(kv[r, cols(h)], finishes[b], 1, 0)).astype(BF16)
         for c in kv_copies(h):
             c.start()
         return carry
@@ -278,7 +286,7 @@
 
     def x_send(d):
         return rcopy(
-            xown.at[lax.rem(x + d, X)], xt.at[x_rows(hd), x_cols(x)],
+            xown.at[x_rows(lax.rem(x + d, X))], xt.at[x_rows(hd), x_cols(x)],
             xs_s.at[d - 1], xs_r.at[d - 1], at_x(d),
         )
 
@@ -287,14 +295,36 @@
         dst = xt.at[x_rows(hd), x_cols(xf)]
         rcopy(dst, dst, xs_s.at[d - 1], xs_r.at[d - 1], at_x(d)).wait_recv()
 
-    def y_send(xi, d):
-        mine = xt.at[x_rows(hd), x_cols(xi)]
-        return rcopy(mine, mine, ys_s.at[xi, d - 1], ys_r.at[xi, d - 1], at_y(d))
-
-    def y_recv(xi, d):
-        owner = lax.rem(y - d + Y, Y) * 2 + core
-        dst = xt.at[x_rows(owner), x_cols(xi)]
-        rcopy(dst, dst, ys_s.at[xi, d - 1], ys_r.at[xi, d - 1], at_y(d)).wait_recv()
+    def y_part(owner_y, xi, half=None):
+        owner = lax.rem(owner_y + Y, Y) * 2 + core
+        if half is None:
+            return xt.at[x_rows(owner), x_cols(xi)]
+        return xt.at[pl.ds(pl.multiple_of(owner * F + half * (F // 2), F // 2), F // 2), x_cols(xi)]
+
+    def y_send(xi, way):
+        mine = y_part(y, xi)
+        return rcopy(mine, mine, ys_s.at[xi, way], ys_r.at[xi, way], at_y(Y - 1 if way else 1))
+
+    def y_recv(xi, way):
+        dst = y_part(y + 1 if way else y - 1, xi)
+        rcopy(dst, dst, ys_s.at[xi, way], ys_r.at[xi, way], at_y(1)).wait_recv()
+
+    def y_pass(xi, way):
+        got = y_part(y + 1 if way else y - 1, xi, way)
+        return rcopy(got, got, yf_s.at[xi, way], yf_r.at[xi, way], at_y(Y - 1 if way else 1))
+
+    def y_pass_recv(xi, way):
+        dst = y_part(y + 2, xi, way)
+        rcopy(dst, dst, yf_s.at[xi, way], yf_r.at[xi, way], at_y(1)).wait_recv()
+
+    def y_start(xi):
+        for way in range(2):
+            y_send(xi, way).start()
+
+    def y_forward(xi):
+        for way in range(2):
+            y_recv(xi, way)
+            y_pass(xi, way).start()
 
     def core_send(d):
         mine = xt.at[x_rows(lax.rem(y - d + Y, Y) * 2 + core)]
@@ -306,52 +336,66 @@
 
     loads[0].wait()
     loads[1].wait()
-    lax.fori_loop(0, H, mem_head, 0)
-    loads[2].wait()
-    for i in range(X):
-        xown[i] = xin[:, i * F : (i + 1) * F].T
+    for h in range(H):
+        mem_head(h, 0)
     pl.semaphore_wait(barrier, len(partners))
     send_stage1(MEM)
-    own = pltpu.make_async_copy(xown.at[x], xt.at[x_rows(hd), x_cols(x)], xl)
+    loads[2].wait()
+    for i in range(X * F // W):
+        xown[i * W : (i + 1) * W] = xin[:, i * W : (i + 1) * W].T
+    own = pltpu.make_async_copy(xown.at[x_rows(x)], xt.at[x_rows(hd), x_cols(x)], xl)
     own.start()
     for d in (1, 3, 2):
         x_send(d).start()
     own.wait()
-    for d in (1, 3, 2):
-        y_send(x, d).start()
+    y_start(x)
     loads[3].wait()
     loads[4].wait()
-    lax.fori_loop(0, H, back_head, 0)
+    for h in range(H):
+        back_head(h, 0)
     send_stage1(BACK)
     for g in range(G):
         line_sums(MEM, g)
-    for g in range(G):
-        line_sums(BACK, g)
-    lax.fori_loop(0, H // 2, inner_head, 0)
-    for d in (1, 3, 2):
+    lax.fori_loop(0, 3, inner_head, 0)
+    for d in (1, 3):
         x_recv(d)
-        for e in (1, 3, 2):
-            y_send(lax.rem(x - d + X, X), e).start()
+        y_start(lax.rem(x - d + X, X))
+    y_forward(x)
+    lax.fori_loop(3, 6, inner_head, 0)
+    x_recv(2)
+    y_start(lax.rem(x + 2, X))
     core_send(0).start()
     for g in range(G):
         scans(MEM, g)
-    lax.fori_loop(H // 2, H, inner_head, 0)
+    y_forward(lax.rem(x + 3, X))
+    for g in range(G):
+        line_sums(BACK, g)
+    lax.fori_loop(6, H, inner_head, 0)
     for g in range(G):
         for d in range(1, X):
             stage3_recv(MEM, g, d)
-        lax.fori_loop(g * HG, (g + 1) * HG, query_head, 0)
-    for g in range(G):
-        scans(BACK, g)
-    for g in range(G):
+        for h in range(g * HG, (g + 1) * HG):
+            query_head(h, 0)
+        y_forward(lax.rem(x + 1 + g, X))
+
+    def keys_values(g):
         for d in range(1, X):
             stage3_recv(BACK, g, d)
         lax.fori_loop(g * HG, (g + 1) * HG, key_value_head, 0)
-    for d in (1, 3, 2):
+
+    def inputs_near():
+        for d in (1, 3):
+            core_send(d).start()
+
+    def inputs_far():
         for xi in range(X):
-            y_recv(xi, d)
-        core_send(d).start()
-    for d in range(Y):
-        core_recv(d)
+            for way in range(2):
+                y_pass_recv(xi, way)
+        core_send(2).start()
+
+    def inputs_all():
+        for d in range(Y):
+            core_recv(d)
 
     def hops(j, way):
         odd = lax.rem(j, 2)
@@ -373,50 +417,88 @@
     def weight_copy(j):
         return pltpu.make_async_copy(wout.at[j], weight_out.at[:, cols(j)], w_o.at[j])
 
+    def product(j, carry):
+        for way in range(2):
+            qg_pass_recv(j, way)
+        for i in range(2):
+            r = pl.ds(i * (FEATURES // 2), FEATURES // 2)
+            part[j, r] = dot(xt[r, :], qg[j], 1, 0)
+        for way in range(2):
+            sb[j, way, 0] = block(j, target(j, way, 0)).astype(BF16)
+            ring(j, way, 0).start()
+        return carry
+
+    def level(s):
+        def one(j, carry):
+            for way in range(2):
+                @pl.when(s < hops(j, way))
+                def _():
+                    ring(j, way, s - 1).wait_recv()
+                    total = rb[j, way, s - 1].astype(F32) + block(j, target(j, way, s))
+                    sb[j, way, s] = total.astype(BF16)
+                    ring(j, way, s).start()
+
+            return carry
+
+        return one
+
+    def finish(j, carry):
+        total = block(j, z)
+        for way in range(2):
+            s = hops(j, way) - 1
+            ring(j, way, s).wait_recv()
+            total += rb[j, way, s].astype(F32)
+        wout[j] = total
+        weight_copy(j).start()
+        return carry
+
     def slot(t, carry):
+        @pl.when(t + LEAD < H)
+        def _():
+            for way in range(2):
+                qg_send(t + LEAD, way).start()
+
         @pl.when(t < H)
         def _():
-            for d in range(1, X):
-                qg_recv(t, d)
-            for i in range(2):
-                r = pl.ds(i * (FEATURES // 2), FEATURES // 2)
-                part[t, r] = dot(xt[r, :], qg[t], 1, 0)
             for way in range(2):
-                sb[t, way, 0] = block(t, target(t, way, 0)).astype(BF16)
-                ring(t, way, 0).start()
-
-        for s in range(1, Z // 2):
-            j = t - s
-
-            @pl.when((j >= 0) & (j < H))
+                qg_recv(t, way)
+                qg_pass(t, way).start()
+
+        @pl.when(t == 0)
+        def _():
+            inputs_near()
+
+        @pl.when(t == FIRST - 1)
+        def _():
+            inputs_far()
+            for g in range(G):
+                scans(BACK, g)
+
+        @pl.when(t == FIRST)
+        def _():
+            inputs_all()
+
+        for s in range(Z // 2, -1, -1):
+            u = t - 1 - s
+            first = (u == FIRST - 1).astype(jnp.int32)
+            low = u - first * (FIRST - 1)
+            high = jnp.where((u >= FIRST - 1) & (u < H), u + 1, low)
+            step = product if s == 0 else finish if s == Z // 2 else level(s)
+            lax.fori_loop(low, high, step, 0)
+
+        for g in range(G):
+            @pl.when(t == FIRST + 1 + g)
             def _():
-                for way in range(2):
-                    @pl.when(s < hops(j, way))
-                    def _():
-                        ring(j, way, s - 1).wait_recv()
-                        total = rb[j, way, s - 1].astype(F32) + block(j, target(j, way, s))
-                        sb[j, way, s] = total.astype(BF16)
-                        ring(j, way, s).start()
-
-        last = t - Z // 2
-
-        @pl.when(last >= 0)
-        def _():
-            total = block(last, z)
-            for way in range(2):
-                s = hops(last, way) - 1
-                ring(last, way, s).wait_recv()
-                total += rb[last, way, s].astype(F32)
-            wout[last] = total
-            weight_copy(last).start()
-
-        return carry
-
-    lax.fori_loop(0, H + Z // 2, slot, 0)
+                keys_values(g)
+
+        return carry
+
+    lax.fori_loop(0, H + 1 + Z // 2, slot, 0)
 
     def drain(h, carry):
-        for d in range(1, X):
-            qg_send(h, d).wait_send()
+        for way in range(2):
+            qg_send(h, way).wait_send()
+            qg_pass(h, way).wait_send()
         for way in range(2):
             for s in range(Z // 2):
                 @pl.when(s < hops(h, way))
@@ -434,9 +516,10 @@
             for g in range(G):
                 stage1(kind, g, d).wait_send()
                 stage3(kind, g, d).wait_send()
-    for d in range(1, Y):
-        for xi in range(X):
-            y_send(xi, d).wait_send()
+    for xi in range(X):
+        for way in range(2):
+            y_send(xi, way).wait_send()
+            y_pass(xi, way).wait_send()
     for d in range(Y):
         core_send(d).wait_send()
     for g in range(G):
@@ -455,11 +538,11 @@
 def local(inputs, query, key_rows, value, grad_out, decay_power):
     dma = pltpu.SemaphoreType.DMA
     anywhere = pl.BlockSpec(memory_space=pl.ANY)
-    return pl.pallas_call(
+    key_grad, value_grad, weight_grad = pl.pallas_call(
         kernel,
         out_shape=(
-            jax.ShapeDtypeStruct((T, H * W), F32),
-            jax.ShapeDtypeStruct((T, H * W), F32),
+            jax.ShapeDtypeStruct((T, H * W), BF16),
+            jax.ShapeDtypeStruct((T, H * W), BF16),
             jax.ShapeDtypeStruct((F, H * W), F32),
         ),
         in_specs=[anywhere] * 5 + [pl.BlockSpec(memory_space=pltpu.SMEM)],
@@ -470,8 +553,9 @@
             pltpu.VMEM((T, H * W), BF16),
             pltpu.VMEM((T, H * W), BF16),
             pltpu.VMEM((T, H * W), BF16),
-            pltpu.VMEM((X, F, T), BF16),
+            pltpu.VMEM((X * F, T), BF16),
             pltpu.VMEM((FEATURES, X * T), BF16),
+            pltpu.VMEM((2, H, 8, W), F32),
             pltpu.VMEM((H, W, W), F32),
             pltpu.VMEM((H, W, W), F32),
             pltpu.VMEM((2, X, H, Q, W), BF16),
@@ -483,6 +567,8 @@
             pltpu.VMEM((H, T, W), F32),
             pltpu.VMEM((H, T, W), F32),
             pltpu.VMEM((H, T, W), F32),
+            pltpu.VMEM((H, T, W), BF16),
+            pltpu.VMEM((H, T, W), BF16),
             pltpu.VMEM((H, X * T, W), BF16),
             pltpu.VMEM((H, FEATURES, W), F32),
             pltpu.VMEM((H, 2, Z // 2, F, W), BF16),
@@ -492,8 +578,10 @@
             dma,
             dma((X - 1,)),
             dma((X - 1,)),
-            dma((X, Y - 1)),
-            dma((X, Y - 1)),
+            dma((X, 2)),
+            dma((X, 2)),
+            dma((X, 2)),
+            dma((X, 2)),
             dma((Y,)),
             dma((Y,)),
             dma((2, G, X - 1)),
@@ -502,8 +590,10 @@
             dma((G, Z)),
             dma((2, G, X - 1)),
             dma((2, G, X - 1)),
-            dma((H, X - 1)),
-            dma((H, X - 1)),
+            dma((H, 2)),
+            dma((H, 2)),
+            dma((H, 2)),
+            dma((H, 2)),
             dma((H, 2, Z // 2)),
             dma((H, 2, Z // 2)),
             dma((2, H)),
@@ -516,6 +606,7 @@
             flops=9 * 10**9, bytes_accessed=10 * 2**20, transcendentals=10**6
         ),
     )(inputs, query, key_rows, value, grad_out, decay_power)
+    return key_grad.astype(F32), value_grad.astype(F32), weight_grad
 
 
 def solution(mesh):

time: 139 us -> 107 us (0.77); the launches traced: 137 us -> 106 us
  Pallas kernels: 130 us -> 100 us
  local copies, waits for them, and re-layouts: 5.87 us -> 0.89 us
  other arithmetic: 0 us -> 4.44 us
    pallas_call x1, Pallas kernels: 130 us -> 100 us  [local(): pl.pallas_call(kernel, out_shape=(jax.ShapeDtypeStruct((T, H * W), BF16),...]
    unnamed x7 -> x5, local copies, waits for them, and re-layouts: 5.87 us -> 0.89 us
    convert_element_type x0 -> x2, other arithmetic: none -> 4.44 us  [local(): return (key_grad.astype(F32), value_grad.astype(F32), weight_grad)]
where the time goes in v2:
time: 107 us; the launch traced here: 106 us
  Pallas kernels  100 us (93%)
  other arithmetic  4.44 us (4%)
    pallas_call x1, Pallas kernels, local(): pl.pallas_call(kernel, out_shape=(jax.ShapeDtypeStruct((T, H * W), BF16),...  100 us
    convert_element_type x2, other arithmetic, local(): return (key_grad.astype(F32), value_grad.astype(F32), weight_grad)  4.44 us

profile of v2, /device:TPU:8, one launch (start us, length us, event | category | flops | bytes accessed | tf_op | source)
XLA Modules:
  0.0 106.4 jit_solution(2565011948614904401)
XLA Ops:
  0.6 100.4 %shard_map.85 = (bf16[512,1024]{1,0:T(8,128)(2,1)}, bf16[512,1024]{1,0:T(8,128)(2,1)}, f32[192,1024]{1,0:T(8,128)}) custom-call(bf16[512,768]{1,0:T(8,128)(2,1)} %x_hbm.1, bf16[512,1024]{1,0:T(8,128)(2,1)} %q_hbm.1, bf16[512,1024]{1,0:T(8,128)(2,1)} %k_hbm.1, bf16[512,1024]{1,0:T(8,128)(2,1)} %v_hbm.1, bf16[512,1024]{1,0:T(8,128)(2,1)} %g_hbm.1, s32[64]{0:T(128)} %power.1), custom_call_target="tpu_custom_call" | custom-call | flops 8999999488 | bytes 10485760 | tf_op jit(solution)/shard_map/pallas_call | solution.py:541
  101.1 0.0 copy-start
  101.1 2.9 %convert_element_type.6 = f32[512,1024]{1,0:T(8,128)} convert(bf16[512,1024]{1,0:T(8,128)(2,1)} %get-tuple-element.6) | non-fusion elementwise | flops 524288 | bytes 3145728 | tf_op jit(solution)/shard_map/convert_element_type | solution.py:609
  104.0 0.0 copy-done
  104.0 0.0 copy-start.1
  104.0 1.6 %convert_element_type.7 = f32[512,1024]{1,0:T(8,128)} convert(bf16[512,1024]{1,0:T(8,128)(2,1)S(1)} %copy-done) | non-fusion elementwise | flops 524288 | bytes 3145728 | tf_op jit(solution)/shard_map/convert_element_type | solution.py:609
  105.5 0.0 copy-done.1
  105.5 0.9 copy.10
Async XLA Ops:
  101.1 2.9 %copy-start = (bf16[512,1024]{1,0:T(8,128)(2,1)S(1)}, bf16[512,1024]{1,0:T(8,128)(2,1)}, u32[]{:S(2)}) copy-start(bf16[512,1024]{1,0:T(8,128)(2,1)} %get-tuple-element.7) | copy-start | bytes 3145732
  104.0 1.6 %copy-start.1 = (f32[192,1024]{1,0:T(8,128)S(1)}, f32[192,1024]{1,0:T(8,128)}, u32[]{:S(2)}) copy-start(f32[192,1024]{1,0:T(8,128)} %get-tuple-element.14) | copy-start | bytes 2359300

commit v3 on v2

--- a/solution.py
+++ b/solution.py
@@ -20,8 +20,8 @@
 MESH = pl.DeviceIdType.MESH
 F32, BF16 = jnp.float32, jnp.bfloat16
 MEM, BACK = 0, 1
-LEAD = 2
-FIRST = 2
+LEAD = 3
+LAG = 2
 
 
 def dot(a, b, ca, cb):
@@ -39,7 +39,7 @@
     key_out, value_out, weight_out,
     xin, qv, kv, vv, gv, xown, xt, fades,
     bm0, bb1, memq, s1, lz, gz, out3, p3,
-    qi, kg, vg, kgo, vgo, qg, part, sb, rb, wout,
+    qi, kgo, vgo, qg, part, sb, rb, wout,
     ld, xl, xs_s, xs_r, ys_s, ys_r, yf_s, yf_r, cs_s, cs_r,
     s1_s, s1_r, s2_s, s2_r, s3_s, s3_r, qg_s, qg_r, qf_s, qf_r, rs_s, rs_r, kv_o, w_o,
 ):
@@ -62,7 +62,7 @@
     loads = [
         pltpu.make_async_copy(src, dst, ld.at[i])
         for i, (src, dst) in enumerate(
-            ((k_hbm, kv), (v_hbm, vv), (x_hbm, xin), (q_hbm, qv), (g_hbm, gv))
+            ((x_hbm, xin), (k_hbm, kv), (v_hbm, vv), (q_hbm, qv), (g_hbm, gv))
         )
     ]
     for c in loads:
@@ -205,22 +205,18 @@
         for d in (1, 3, 2):
             stage3(kind, g, d).start()
 
-    def inner_head(h, carry):
-        rate = rate_of(h)
+    def gaps():
         t = lax.broadcasted_iota(jnp.int32, (B, B), 0)
         s = lax.broadcasted_iota(jnp.int32, (B, B), 1)
-        gap = (t - s).astype(F32)
-        fade = jnp.where(gap >= 0.0, jnp.exp(-rate * jnp.maximum(gap, 0.0)), 0.0)
-        turned = jnp.where(gap <= 0.0, jnp.exp(rate * jnp.minimum(gap, 0.0)), 0.0)
+        return (t - s).astype(F32)
+
+    def inner_head(h, carry):
+        gap = gaps()
+        fade = jnp.where(gap >= 0.0, jnp.exp(-rate_of(h) * jnp.maximum(gap, 0.0)), 0.0)
         for b in range(2):
             r = pl.ds(b * B, B)
-            qh, kh, vh, gh = (a[r, cols(h)] for a in (qv, kv, vv, gv))
-            sa = (dot(gh, vh, 1, 1) * fade).astype(BF16)
-            qi[h, r] = dot(sa, kh, 1, 0)
-            sat = (dot(vh, gh, 1, 1) * turned).astype(BF16)
-            kg[h, r] = dot(sat, qh, 1, 0)
-            sbt = (dot(kh, qh, 1, 1) * turned).astype(BF16)
-            vg[h, r] = dot(sbt, gh, 1, 0)
+            sa = (dot(gv[r, cols(h)], vv[r, cols(h)], 1, 1) * fade).astype(BF16)
+            qi[h, r] = dot(sa, kv[r, cols(h)], 1, 0)
         return carry
 
     def line(xi, half=None):
@@ -267,13 +263,18 @@
 
     def key_value_head(h, carry):
         rate = rate_of(h)
+        gap = gaps()
+        turned = jnp.where(gap <= 0.0, jnp.exp(rate * jnp.minimum(gap, 0.0)), 0.0)
         fall = jnp.exp(-rate * (float(B) - rows()))
         suffix = p3[BACK, :, h].reshape(W, W)
         finishes = ((decay(rate, float(B)) * suffix.astype(F32) + bb1[h]).astype(BF16), suffix)
         for b in range(2):
             r = pl.ds(b * B, B)
-            kgo[h, r] = (kg[h, r] + fall * dot(vv[r, cols(h)], finishes[b], 1, 1)).astype(BF16)
-            vgo[h, r] = (vg[h, r] + fall * dot(kv[r, cols(h)], finishes[b], 1, 0)).astype(BF16)
+            qh, kh, vh, gh = (a[r, cols(h)] for a in (qv, kv, vv, gv))
+            sat = (dot(vh, gh, 1, 1) * turned).astype(BF16)
+            kgo[h, r] = (dot(sat, qh, 1, 0) + fall * dot(vh, finishes[b], 1, 1)).astype(BF16)
+            sbt = (dot(kh, qh, 1, 1) * turned).astype(BF16)
+            vgo[h, r] = (dot(sbt, gh, 1, 0) + fall * dot(kh, finishes[b], 1, 0)).astype(BF16)
         for c in kv_copies(h):
             c.start()
         return carry
@@ -326,6 +327,14 @@
             y_recv(xi, way)
             y_pass(xi, way).start()
 
+    def y_far(xi):
+        mine = y_part(y, xi)
+        return rcopy(mine, mine, yf_s.at[xi, 0], yf_r.at[xi, 0], at_y(2))
+
+    def y_far_recv(xi):
+        dst = y_part(y + 2, xi)
+        rcopy(dst, dst, yf_s.at[xi, 0], yf_r.at[xi, 0], at_y(2)).wait_recv()
+
     def core_send(d):
         mine = xt.at[x_rows(lax.rem(y - d + Y, Y) * 2 + core)]
         return rcopy(mine, mine, cs_s.at[d], cs_r.at[d], sibling)
@@ -335,17 +344,17 @@
         rcopy(dst, dst, cs_s.at[d], cs_r.at[d], sibling).wait_recv()
 
     loads[0].wait()
+    for i in range(X * F // W):
+        xown[i * W : (i + 1) * W] = xin[:, i * W : (i + 1) * W].T
     loads[1].wait()
+    loads[2].wait()
     for h in range(H):
         mem_head(h, 0)
     pl.semaphore_wait(barrier, len(partners))
     send_stage1(MEM)
-    loads[2].wait()
-    for i in range(X * F // W):
-        xown[i * W : (i + 1) * W] = xin[:, i * W : (i + 1) * W].T
     own = pltpu.make_async_copy(xown.at[x_rows(x)], xt.at[x_rows(hd), x_cols(x)], xl)
     own.start()
-    for d in (1, 3, 2):
+    for d in (1, 3):
         x_send(d).start()
     own.wait()
     y_start(x)
@@ -353,30 +362,29 @@
     loads[4].wait()
     for h in range(H):
         back_head(h, 0)
-    send_stage1(BACK)
-    for g in range(G):
-        line_sums(MEM, g)
-    lax.fori_loop(0, 3, inner_head, 0)
+    line_sums(MEM, 0)
+    lax.fori_loop(0, H // 2, inner_head, 0)
+    x_send(2).start()
+    y_forward(x)
     for d in (1, 3):
         x_recv(d)
         y_start(lax.rem(x - d + X, X))
-    y_forward(x)
-    lax.fori_loop(3, 6, inner_head, 0)
+    line_sums(MEM, 1)
+    send_stage1(BACK)
+    lax.fori_loop(H // 2, H, inner_head, 0)
     x_recv(2)
     y_start(lax.rem(x + 2, X))
+    y_far(lax.rem(x + 2, X)).start()
     core_send(0).start()
-    for g in range(G):
-        scans(MEM, g)
+    scans(MEM, 0)
     y_forward(lax.rem(x + 3, X))
-    for g in range(G):
-        line_sums(BACK, g)
-    lax.fori_loop(6, H, inner_head, 0)
-    for g in range(G):
+    y_forward(lax.rem(x + 1, X))
+
+    def queries(g):
         for d in range(1, X):
             stage3_recv(MEM, g, d)
         for h in range(g * HG, (g + 1) * HG):
             query_head(h, 0)
-        y_forward(lax.rem(x + 1 + g, X))
 
     def keys_values(g):
         for d in range(1, X):
@@ -388,14 +396,23 @@
             core_send(d).start()
 
     def inputs_far():
-        for xi in range(X):
+        for d in (0, 1, 3):
             for way in range(2):
-                y_pass_recv(xi, way)
+                y_pass_recv(lax.rem(x + d, X), way)
+        y_far_recv(lax.rem(x + 2, X))
         core_send(2).start()
 
     def inputs_all():
         for d in range(Y):
             core_recv(d)
+
+    queries(0)
+    scans(MEM, 1)
+    for g in range(G):
+        line_sums(BACK, g)
+    for way in range(2):
+        y_recv(lax.rem(x + 2, X), way)
+    inputs_near()
 
     def hops(j, way):
         odd = lax.rem(j, 2)
@@ -466,34 +483,37 @@
 
         @pl.when(t == 0)
         def _():
-            inputs_near()
-
-        @pl.when(t == FIRST - 1)
+            queries(1)
+
+        @pl.when(t == 1)
         def _():
             inputs_far()
+
+        @pl.when(t == LAG)
+        def _():
+            inputs_all()
+
+        for s in range(Z // 2 + 1):
+            j = t - LAG * (s + 1)
+            step = product if s == 0 else finish if s == Z // 2 else level(s)
+
+            @pl.when((j >= 0) & (j < H))
+            def _():
+                step(j, 0)
+
+        @pl.when(t == H - LEAD)
+        def _():
             for g in range(G):
                 scans(BACK, g)
 
-        @pl.when(t == FIRST)
-        def _():
-            inputs_all()
-
-        for s in range(Z // 2, -1, -1):
-            u = t - 1 - s
-            first = (u == FIRST - 1).astype(jnp.int32)
-            low = u - first * (FIRST - 1)
-            high = jnp.where((u >= FIRST - 1) & (u < H), u + 1, low)
-            step = product if s == 0 else finish if s == Z // 2 else level(s)
-            lax.fori_loop(low, high, step, 0)
-
         for g in range(G):
-            @pl.when(t == FIRST + 1 + g)
+            @pl.when(t == H + LAG * (g + 1))
             def _():
                 keys_values(g)
 
         return carry
 
-    lax.fori_loop(0, H + 1 + Z // 2, slot, 0)
+    lax.fori_loop(0, H + LAG * (1 + Z // 2), slot, 0)
 
     def drain(h, carry):
         for way in range(2):
@@ -519,7 +539,10 @@
     for xi in range(X):
         for way in range(2):
             y_send(xi, way).wait_send()
-            y_pass(xi, way).wait_send()
+    for d in (0, 1, 3):
+        for way in range(2):
+            y_pass(lax.rem(x + d, X), way).wait_send()
+    y_far(lax.rem(x + 2, X)).wait_send()
     for d in range(Y):
         core_send(d).wait_send()
     for g in range(G):
@@ -533,6 +556,30 @@
 
         lax.fori_loop(z + 1, Z, up, 0)
         lax.fori_loop(0, z, down, 0)
+
+
+def widen_kernel(key_low, value_low, weight, key_out, value_out, weight_out):
+    key_out[...] = key_low[...].astype(F32)
+    value_out[...] = value_low[...].astype(F32)
+    weight_out[...] = weight[...]
+
+
+def widen(key_grad, value_grad, weight_grad):
+    steps = 8
+    tall = pl.BlockSpec((T // steps, H * W), lambda i: (i, 0))
+    low = pl.BlockSpec((F // steps, H * W), lambda i: (i, 0))
+    return pl.pallas_call(
+        widen_kernel,
+        grid=(steps,),
+        out_shape=(
+            jax.ShapeDtypeStruct((T, H * W), F32),
+            jax.ShapeDtypeStruct((T, H * W), F32),
+            jax.ShapeDtypeStruct((F, H * W), F32),
+        ),
+        in_specs=[tall, tall, low],
+        out_specs=(tall, tall, low),
+        compiler_params=pltpu.CompilerParams(vmem_limit_bytes=60 * 2**20),
+    )(key_grad, value_grad, weight_grad)
 
 
 def local(inputs, query, key_rows, value, grad_out, decay_power):
@@ -564,8 +611,6 @@
             pltpu.VMEM((Z, H, Q, W), BF16),
             pltpu.VMEM((2, X, H, Q, W), BF16),
             pltpu.VMEM((2, X, H, Q, W), BF16),
-            pltpu.VMEM((H, T, W), F32),
-            pltpu.VMEM((H, T, W), F32),
             pltpu.VMEM((H, T, W), F32),
             pltpu.VMEM((H, T, W), BF16),
             pltpu.VMEM((H, T, W), BF16),
@@ -606,7 +651,7 @@
             flops=9 * 10**9, bytes_accessed=10 * 2**20, transcendentals=10**6
         ),
     )(inputs, query, key_rows, value, grad_out, decay_power)
-    return key_grad.astype(F32), value_grad.astype(F32), weight_grad
+    return widen(key_grad, value_grad, weight_grad)
 
 
 def solution(mesh):

time: 107 us -> 104 us (0.972)
  the two profiles are of different devices: /device:TPU:8 before, /device:TPU:38 now
where the time goes in v3:
time: 104 us
  Pallas kernels  103 us (99%)
    pallas_call x1, Pallas kernels, local(): pl.pallas_call(kernel, out_shape=(jax.ShapeDtypeStruct((T, H * W), BF16),...  96.8 us
    pallas_call x1, Pallas kernels, widen(): pl.pallas_call(widen_kernel, grid=(steps,), out_shape=(jax.ShapeDtypeStru...  6.72 us

profile of v3, /device:TPU:38, one launch (start us, length us, event | category | flops | bytes accessed | tf_op | source)
XLA Modules:
  0.0 104.1 jit_solution(2370015917575533116)
XLA Ops:
  0.6 96.8 %shard_map.85 = (bf16[512,1024]{1,0:T(8,128)(2,1)}, bf16[512,1024]{1,0:T(8,128)(2,1)}, f32[192,1024]{1,0:T(8,128)}) custom-call(bf16[512,768]{1,0:T(8,128)(2,1)} %x_hbm.1, bf16[512,1024]{1,0:T(8,128)(2,1)} %q_hbm.1, bf16[512,1024]{1,0:T(8,128)(2,1)} %k_hbm.1, bf16[512,1024]{1,0:T(8,128)(2,1)} %v_hbm.1, bf16[512,1024]{1,0:T(8,128)(2,1)} %g_hbm.1, s32[64]{0:T(128)} %power.1), custom_call_target="tpu_custom_call" | custom-call | flops 8999999488 | bytes 10485760 | tf_op jit(solution)/shard_map/pallas_call | solution.py:588
  97.4 6.7 %shard_map.86 = (f32[512,1024]{1,0:T(8,128)}, f32[512,1024]{1,0:T(8,128)}, f32[192,1024]{1,0:T(8,128)}) custom-call(bf16[512,1024]{1,0:T(8,128)(2,1)} %get-tuple-element.6.key_low, bf16[512,1024]{1,0:T(8,128)(2,1)} %get-tuple-element.7.value_low, f32[192,1024]{1,0:T(8,128)} %get-tuple-element.8.weight), custom_call_target="tpu_custom_call" | custom-call | tf_op jit(solution)/shard_map/pallas_call | solution.py:571
